TPU v7x, 32 devices: a whole 2x2x4 slice. The times are simulated.
32 devices in a mesh: group: 2 (over y), inline: 4 (over z), xline: 2 (over core), shot: 2 (over x).
Axes of the slice: x: 2, y: 2, z: 4, core: 2. Of those that a mesh axis runs over, the one named last changes fastest.
Arguments:
- vel2: float32 [64, 32, 128], P('inline', 'xline'), may hold values from 0.05 to 0.18
- adj_prev: float32 [4, 64, 32, 128], P(('group', 'shot'), 'inline', 'xline'), parts along dimension 0, may hold values from -6 to 6
- adj_now: float32 [4, 64, 32, 128], P(('group', 'shot'), 'inline', 'xline'), parts along dimension 0, may hold values from -6 to 6
- src_field: float32 [4, 8, 64, 32, 128], P(('group', 'shot'), None, 'inline', 'xline'), parts along dimension 0, may hold values from -6 to 6
- residual: float32 [4, 8, 1024], P(('group', 'shot')), parts along dimension 0, may hold values from -18 to 18
- rec_inline: int32 [4, 1024], P(('group', 'shot')), parts along dimension 0, may hold values from 0 to 63
- rec_xline: int32 [4, 1024], P(('group', 'shot')), parts along dimension 0, may hold values from 0 to 31
- src_inline: int32 [4], P(('group', 'shot')), parts along dimension 0, may hold values from 0 to 63
- src_xline: int32 [4], P(('group', 'shot')), parts along dimension 0, may hold values from 0 to 31
- lag_list: int32 [32], replicated, may hold values from -16 to 15, as said below
Outputs:
- dso_image: float32 [64, 64, 32, 128], P(('group', 'shot'), 'inline', 'xline'), parts along dimension 0
There are 2 independent parts, one for each index of `group`. A program takes and returns all parts, laid end to end along the dimension named above; an argument that names none is the same for every part. Nothing has to cross between parts.
Inputs may be any that keep to these rules, and one draw needn't show every extreme that they name: lag_list holds each of the 32 offsets -16 .. 15 once, in an order drawn from the seed.
All inputs are finite; a program needn't handle non-finite values.
Results may differ from a plain program's by a relative error of at most 0.0003.
Values sent between devices are 32-bit elements; how exact they have to be, the bound alone decides.
A program may use at most 128 MiB of HBM per device.

v0:
```python
import jax
import jax.numpy as jnp
from jax import lax
from jax.sharding import PartitionSpec as P

NLAG = 32


stencil_weights = (-205.0 / 72.0, 8.0 / 5.0, -1.0 / 5.0, 8.0 / 315.0, -1.0 / 560.0)
mute_reach = 3
receiver_depth = 1


def with_halo(block, sides, width):
    for axis, dim in sides:
        count = lax.axis_size(axis)
        forward = [(i, i + 1) for i in range(count - 1)]
        backward = [(target, source) for source, target in forward]
        low = lax.ppermute(
            lax.slice_in_dim(block, block.shape[dim] - width, None, axis=dim), axis, forward
        )
        high = lax.ppermute(lax.slice_in_dim(block, 0, width, axis=dim), axis, backward)
        block = jnp.concatenate([low, block, high], axis=dim)
    return block


def stencil(padded):
    size_a, size_b, size_c = padded.shape
    centre = padded[4 : size_a - 4, 4 : size_b - 4, 4 : size_c - 4]
    summed_up = 3.0 * stencil_weights[0] * centre
    for reach in range(1, 5):
        summed_up = summed_up + stencil_weights[reach] * (
            padded[4 + reach : size_a - 4 + reach, 4 : size_b - 4, 4 : size_c - 4]
            + padded[4 - reach : size_a - 4 - reach, 4 : size_b - 4, 4 : size_c - 4]
            + padded[4 : size_a - 4, 4 + reach : size_b - 4 + reach, 4 : size_c - 4]
            + padded[4 : size_a - 4, 4 - reach : size_b - 4 - reach, 4 : size_c - 4]
            + padded[4 : size_a - 4, 4 : size_b - 4, 4 + reach : size_c - 4 + reach]
            + padded[4 : size_a - 4, 4 : size_b - 4, 4 - reach : size_c - 4 - reach]
        )
    return summed_up


def on_device(
    vel2,
    adj_prev,
    adj_now,
    src_field,
    residual,
    rec_inline,
    rec_xline,
    src_inline,
    src_xline,
    lag_list,
):
    lag_reach = NLAG // 2
    cell_rows, cell_cols, depth_cells = vel2.shape
    step_count = src_field.shape[1]
    row_cells = lax.axis_index("inline") * cell_rows + jnp.arange(cell_rows, dtype=jnp.int32)
    col_cells = lax.axis_index("xline") * cell_cols + jnp.arange(cell_cols, dtype=jnp.int32)
    inside = (jnp.abs(row_cells[:, None] - src_inline[0]) <= mute_reach) & (
        jnp.abs(col_cells[None, :] - src_xline[0]) <= mute_reach
    )
    mute_mask = 1.0 - inside.astype(jnp.float32)
    depth_mask = (jnp.arange(depth_cells, dtype=jnp.int32) == receiver_depth).astype(jnp.float32)
    hit_rows = (rec_inline[0][:, None] == row_cells[None, :]).astype(jnp.float32)
    hit_cols = (rec_xline[0][:, None] == col_cells[None, :]).astype(jnp.float32)
    own_count = NLAG // lax.axis_size("shot")
    own_lags = lax.dynamic_slice_in_dim(lag_list, lax.axis_index("shot") * own_count, own_count)
    accumulated = jnp.zeros((NLAG, cell_rows, cell_cols, depth_cells), jnp.float32)
    older = adj_prev[0]
    current = adj_now[0]
    for step in range(step_count):
        padded_rim = with_halo(current, (("inline", 0), ("xline", 1)), 4)
        weighted = hit_rows * residual[0, step][:, None]
        surface = jnp.dot(
            weighted.T,
            hit_cols,
            precision=lax.Precision.HIGHEST,
            preferred_element_type=jnp.float32,
        )
        padded = jnp.pad(padded_rim, ((0, 0), (0, 0), (4, 4)))
        advanced = (
            2.0 * current - older + vel2 * (stencil(padded) + surface[:, :, None] * depth_mask)
        )
        lag_view = with_halo(advanced, (("inline", 0),), lag_reach)
        source = src_field[0, step] * mute_mask[:, :, None]

        def one_lag(offset):
            return lax.dynamic_slice_in_dim(lag_view, offset + lag_reach, cell_rows, 0)

        accumulated = accumulated + source[None] * jax.vmap(one_lag)(lag_list)
        older, current = (current, advanced)
    summed = lax.psum_scatter(accumulated, "shot", scatter_dimension=0, tiled=True)
    weights = jnp.abs(own_lags).astype(jnp.float32)
    return summed * weights[:, None, None, None]


def solution(mesh):
    in_specs = (
        P("inline", "xline", None),
        P(("group", "shot"), "inline", "xline", None),
        P(("group", "shot"), "inline", "xline", None),
        P(("group", "shot"), None, "inline", "xline", None),
        P(("group", "shot"), None, None),
        P(("group", "shot"), None),
        P(("group", "shot"), None),
        P(("group", "shot")),
        P(("group", "shot")),
        P(),
    )
    out_specs = P(("group", "shot"), "inline", "xline", None)
    return jax.shard_map(
        on_device, mesh=mesh, in_specs=in_specs, out_specs=out_specs, check_vma=False
    )
```

profile of v0, /device:TPU:0, one launch (start us, length us, event | category | flops | bytes accessed | tf_op | source)
XLA Modules:
  0.0 268.9 jit_solution(31604372693035770)
XLA Ops:
  8.7 5.6 %collective-permute-start.1 = (f32[4,16,128]{2,1,0:T(8,128)S(1)}, f32[4,16,128]{2,1,0:T(8,128)S(1)}, u32[]{:S(2)}, u32[]{:S(2)}) collective-permute-start(f32[4,16,128]{2,1,0:T(8,128)S(1)} %get-tuple-element.60), channel_id=1, source_target_pairs={{0,4},{4,8},{8,12},{1,5},{5,9},{9,13},{2,6},{6,10},{10,14},{3,7},{... | collective-permute-start | bytes 98312 | tf_op jit(solution)/shard_map/ppermute | solution.py:19
  20.7 3.0 %collective-permute-start.3 = (f32[24,4,128]{2,1,0:T(4,128)S(1)}, f32[24,4,128]{2,1,0:T(4,128)S(1)}, u32[]{:S(2)}, u32[]{:S(2)}) collective-permute-start(f32[24,4,128]{2,1,0:T(4,128)S(1)} %get-tuple-element.43), channel_id=1, source_target_pairs={{0,2},{1,3},{4,6},{5,7},{8,10},{9,11},{12,14},{13,15},{16,18},{17,... | collective-permute-start | bytes 147464 | tf_op jit(solution)/shard_map/ppermute | solution.py:19
  30.3 4.6 %collective-permute-start.7 = (f32[4,16,128]{2,1,0:T(8,128)S(1)}, f32[4,16,128]{2,1,0:T(8,128)S(1)}, u32[]{:S(2)}, u32[]{:S(2)}) collective-permute-start(f32[4,16,128]{2,1,0:T(8,128)S(1)} %get-tuple-element.58), channel_id=1, source_target_pairs={{0,4},{4,8},{8,12},{1,5},{5,9},{9,13},{2,6},{6,10},{10,14},{3,7},{... | collective-permute-start | bytes 98312 | tf_op jit(solution)/shard_map/ppermute | solution.py:19
  37.7 3.0 %collective-permute-start.9 = (f32[24,4,128]{2,1,0:T(4,128)S(1)}, f32[24,4,128]{2,1,0:T(4,128)S(1)}, u32[]{:S(2)}, u32[]{:S(2)}) collective-permute-start(f32[24,4,128]{2,1,0:T(4,128)S(1)} %get-tuple-element.39), channel_id=1, source_target_pairs={{0,2},{1,3},{4,6},{5,7},{8,10},{9,11},{12,14},{13,15},{16,18},{17,... | collective-permute-start | bytes 147464 | tf_op jit(solution)/shard_map/ppermute | solution.py:19
  43.9 4.9 %collective-permute-start.13 = (f32[4,16,128]{2,1,0:T(8,128)S(1)}, f32[4,16,128]{2,1,0:T(8,128)S(1)}, u32[]{:S(2)}, u32[]{:S(2)}) collective-permute-start(f32[4,16,128]{2,1,0:T(8,128)S(1)} %get-tuple-element.56), channel_id=1, source_target_pairs={{0,4},{4,8},{8,12},{1,5},{5,9},{9,13},{2,6},{6,10},{10,14},{3,7},{... | collective-permute-start | bytes 98312 | tf_op jit(solution)/shard_map/ppermute | solution.py:19
  51.7 3.0 %collective-permute-start.15 = (f32[24,4,128]{2,1,0:T(4,128)S(1)}, f32[24,4,128]{2,1,0:T(4,128)S(1)}, u32[]{:S(2)}, u32[]{:S(2)}) collective-permute-start(f32[24,4,128]{2,1,0:T(4,128)S(1)} %get-tuple-element.35), channel_id=1, source_target_pairs={{0,2},{1,3},{4,6},{5,7},{8,10},{9,11},{12,14},{13,15},{16,18},{17,... | collective-permute-start | bytes 147464 | tf_op jit(solution)/shard_map/ppermute | solution.py:19
  57.8 4.9 %collective-permute-start.19 = (f32[4,16,128]{2,1,0:T(8,128)S(1)}, f32[4,16,128]{2,1,0:T(8,128)S(1)}, u32[]{:S(2)}, u32[]{:S(2)}) collective-permute-start(f32[4,16,128]{2,1,0:T(8,128)S(1)} %get-tuple-element.54), channel_id=1, source_target_pairs={{0,4},{4,8},{8,12},{1,5},{5,9},{9,13},{2,6},{6,10},{10,14},{3,7},{... | collective-permute-start | bytes 98312 | tf_op jit(solution)/shard_map/ppermute | solution.py:19
  65.6 3.0 %collective-permute-start.21 = (f32[24,4,128]{2,1,0:T(4,128)S(1)}, f32[24,4,128]{2,1,0:T(4,128)S(1)}, u32[]{:S(2)}, u32[]{:S(2)}) collective-permute-start(f32[24,4,128]{2,1,0:T(4,128)S(1)} %get-tuple-element.31), channel_id=1, source_target_pairs={{0,2},{1,3},{4,6},{5,7},{8,10},{9,11},{12,14},{13,15},{16,18},{17,... | collective-permute-start | bytes 147464 | tf_op jit(solution)/shard_map/ppermute | solution.py:19
  71.7 4.9 %collective-permute-start.25 = (f32[4,16,128]{2,1,0:T(8,128)S(1)}, f32[4,16,128]{2,1,0:T(8,128)S(1)}, u32[]{:S(2)}, u32[]{:S(2)}) collective-permute-start(f32[4,16,128]{2,1,0:T(8,128)S(1)} %get-tuple-element.52), channel_id=1, source_target_pairs={{0,4},{4,8},{8,12},{1,5},{5,9},{9,13},{2,6},{6,10},{10,14},{3,7},{... | collective-permute-start | bytes 98312 | tf_op jit(solution)/shard_map/ppermute | solution.py:19
  83.6 4.2 %collective-permute-start.4 = (f32[16,16,128]{2,1,0:T(8,128)S(1)}, f32[16,16,128]{2,1,0:T(8,128)S(1)}, u32[]{:S(2)}, u32[]{:S(2)}) collective-permute-start(f32[16,16,128]{2,1,0:T(8,128)S(1)} %fusion.293), channel_id=1, source_target_pairs={{0,4},{4,8},{8,12},{1,5},{5,9},{9,13},{2,6},{6,10},{10,14},{3,7},{... | collective-permute-start | bytes 393224 | tf_op jit(solution)/shard_map/ppermute | solution.py:19
  91.2 5.2 %collective-permute-start.31 = (f32[4,16,128]{2,1,0:T(8,128)S(1)}, f32[4,16,128]{2,1,0:T(8,128)S(1)}, u32[]{:S(2)}, u32[]{:S(2)}) collective-permute-start(f32[4,16,128]{2,1,0:T(8,128)S(1)} %get-tuple-element.50), channel_id=1, source_target_pairs={{0,4},{4,8},{8,12},{1,5},{5,9},{9,13},{2,6},{6,10},{10,14},{3,7},{... | collective-permute-start | bytes 98312 | tf_op jit(solution)/shard_map/ppermute | solution.py:19
  96.4 3.9 %collective-permute-start.10 = (f32[16,16,128]{2,1,0:T(8,128)S(1)}, f32[16,16,128]{2,1,0:T(8,128)S(1)}, u32[]{:S(2)}, u32[]{:S(2)}) collective-permute-start(f32[16,16,128]{2,1,0:T(8,128)S(1)} %fusion.262), channel_id=1, source_target_pairs={{0,4},{4,8},{8,12},{1,5},{5,9},{9,13},{2,6},{6,10},{10,14},{3,7},{... | collective-permute-start | bytes 393224 | tf_op jit(solution)/shard_map/ppermute | solution.py:19
  103.0 3.2 %collective-permute-start.33 = (f32[24,4,128]{2,1,0:T(4,128)S(1)}, f32[24,4,128]{2,1,0:T(4,128)S(1)}, u32[]{:S(2)}, u32[]{:S(2)}) collective-permute-start(f32[24,4,128]{2,1,0:T(4,128)S(1)} %get-tuple-element.23), channel_id=1, source_target_pairs={{0,2},{1,3},{4,6},{5,7},{8,10},{9,11},{12,14},{13,15},{16,18},{17,... | collective-permute-start | bytes 147464 | tf_op jit(solution)/shard_map/ppermute | solution.py:19
  109.2 4.5 %collective-permute-start.16 = (f32[16,16,128]{2,1,0:T(8,128)S(1)}, f32[16,16,128]{2,1,0:T(8,128)S(1)}, u32[]{:S(2)}, u32[]{:S(2)}) collective-permute-start(f32[16,16,128]{2,1,0:T(8,128)S(1)} %fusion.231), channel_id=1, source_target_pairs={{0,4},{4,8},{8,12},{1,5},{5,9},{9,13},{2,6},{6,10},{10,14},{3,7},{... | collective-permute-start | bytes 393224 | tf_op jit(solution)/shard_map/ppermute | solution.py:19
  117.1 5.2 %collective-permute-start.37 = (f32[4,16,128]{2,1,0:T(8,128)S(1)}, f32[4,16,128]{2,1,0:T(8,128)S(1)}, u32[]{:S(2)}, u32[]{:S(2)}) collective-permute-start(f32[4,16,128]{2,1,0:T(8,128)S(1)} %get-tuple-element.48), channel_id=1, source_target_pairs={{0,4},{4,8},{8,12},{1,5},{5,9},{9,13},{2,6},{6,10},{10,14},{3,7},{... | collective-permute-start | bytes 98312 | tf_op jit(solution)/shard_map/ppermute | solution.py:19
  125.2 3.9 %collective-permute-start.22 = (f32[16,16,128]{2,1,0:T(8,128)S(1)}, f32[16,16,128]{2,1,0:T(8,128)S(1)}, u32[]{:S(2)}, u32[]{:S(2)}) collective-permute-start(f32[16,16,128]{2,1,0:T(8,128)S(1)} %fusion.200), channel_id=1, source_target_pairs={{0,4},{4,8},{8,12},{1,5},{5,9},{9,13},{2,6},{6,10},{10,14},{3,7},{... | collective-permute-start | bytes 393224 | tf_op jit(solution)/shard_map/ppermute | solution.py:19
  137.7 4.5 %collective-permute-start.28 = (f32[16,16,128]{2,1,0:T(8,128)S(1)}, f32[16,16,128]{2,1,0:T(8,128)S(1)}, u32[]{:S(2)}, u32[]{:S(2)}) collective-permute-start(f32[16,16,128]{2,1,0:T(8,128)S(1)} %fusion.169), channel_id=1, source_target_pairs={{0,4},{4,8},{8,12},{1,5},{5,9},{9,13},{2,6},{6,10},{10,14},{3,7},{... | collective-permute-start | bytes 393224 | tf_op jit(solution)/shard_map/ppermute | solution.py:19
  145.6 5.2 %collective-permute-start.43 = (f32[4,16,128]{2,1,0:T(8,128)S(1)}, f32[4,16,128]{2,1,0:T(8,128)S(1)}, u32[]{:S(2)}, u32[]{:S(2)}) collective-permute-start(f32[4,16,128]{2,1,0:T(8,128)S(1)} %get-tuple-element.46), channel_id=1, source_target_pairs={{0,4},{4,8},{8,12},{1,5},{5,9},{9,13},{2,6},{6,10},{10,14},{3,7},{... | collective-permute-start | bytes 98312 | tf_op jit(solution)/shard_map/ppermute | solution.py:19
  153.6 3.9 %collective-permute-start.34 = (f32[16,16,128]{2,1,0:T(8,128)S(1)}, f32[16,16,128]{2,1,0:T(8,128)S(1)}, u32[]{:S(2)}, u32[]{:S(2)}) collective-permute-start(f32[16,16,128]{2,1,0:T(8,128)S(1)} %fusion.138), channel_id=1, source_target_pairs={{0,4},{4,8},{8,12},{1,5},{5,9},{9,13},{2,6},{6,10},{10,14},{3,7},{... | collective-permute-start | bytes 393224 | tf_op jit(solution)/shard_map/ppermute | solution.py:19
  166.2 4.5 %collective-permute-start.40 = (f32[16,16,128]{2,1,0:T(8,128)S(1)}, f32[16,16,128]{2,1,0:T(8,128)S(1)}, u32[]{:S(2)}, u32[]{:S(2)}) collective-permute-start(f32[16,16,128]{2,1,0:T(8,128)S(1)} %fusion.107), channel_id=1, source_target_pairs={{0,4},{4,8},{8,12},{1,5},{5,9},{9,13},{2,6},{6,10},{10,14},{3,7},{... | collective-permute-start | bytes 393224 | tf_op jit(solution)/shard_map/ppermute | solution.py:19
  172.8 4.6 %collective-permute-start.46 = (f32[16,16,128]{2,1,0:T(8,128)S(1)}, f32[16,16,128]{2,1,0:T(8,128)S(1)}, u32[]{:S(2)}, u32[]{:S(2)}) collective-permute-start(f32[16,16,128]{2,1,0:T(8,128)S(1)} %fusion.76), channel_id=1, source_target_pairs={{0,4},{4,8},{8,12},{1,5},{5,9},{9,13},{2,6},{6,10},{10,14},{3,7},{... | collective-permute-start | bytes 393224 | tf_op jit(solution)/shard_map/ppermute | solution.py:19
  187.2 15.0 %multiply_add_fusion = f32[32,16,16,128]{3,2,1,0:T(8,128)} fusion(f32[32,16,16,128]{3,2,1,0:T(8,128)} %gather_fusion.7, f32[32,16,16,128]{3,2,1,0:T(8,128)} %gather_fusion.6, f32[32,16,16,128]{3,2,1,0:T(8,128)} %gather_fusion.5, f32[32,16,16,128]{3,2,1,0:T(8,128)} %gather_fusion.4, f32[32,16,16,128]{3,2,1,0:T(8,128)} %gather_fusion.3, ...), kind=kLoop, calls=%fused_computation.8 | loop fusion | flops 15728640 | bytes 38797312 | tf_op jit(solution)/shard_map/add | solution.py:91
  202.4 56.5 %reduce-scatter.2.cloned.1.call-done = f32[16,16,16,128]{3,2,1,0:T(8,128)} async-done(((f32[32,16,16,128]{3,2,1,0:T(8,128)}), f32[16,16,16,128]{3,2,1,0:T(8,128)}) %reduce-scatter.2.cloned.1.call-update) | async-done | bytes 2097168 | tf_op jit(solution)/shard_map/reduce_scatter | solution.py:93
  258.9 3.2 %broadcast_multiply_fusion = f32[16,16,16,128]{3,2,1,0:T(8,128)} fusion(f32[16,16,16,128]{3,2,1,0:T(8,128)} %reduce-scatter.2.cloned.1.call-done, f32[16]{0:T(128)S(1)} %abs_convert_fusion), kind=kLoop, calls=%fused_computation.33 | loop fusion | flops 524288 | bytes 4194368 | tf_op jit(solution)/shard_map/mul | solution.py:95
  (161 shorter events, 88.7 us)
Async XLA Ops:
  6.5 252.4 %reduce-scatter.2.cloned.1.call-start = ((), (), s32[]{:S(2)}) async-start(), calls=%async_computation.1 | async-start | bytes 6291456 | tf_op jit(solution)/shard_map/reduce_scatter | solution.py:93
  83.6 19.4 %collective-permute-start.4 = (f32[16,16,128]{2,1,0:T(8,128)S(1)}, f32[16,16,128]{2,1,0:T(8,128)S(1)}, u32[]{:S(2)}, u32[]{:S(2)}) collective-permute-start(f32[16,16,128]{2,1,0:T(8,128)S(1)} %fusion.293), channel_id=1, source_target_pairs={{0,4},{4,8},{8,12},{1,5},{5,9},{9,13},{2,6},{6,10},{10,14},{3,7},{... | collective-permute-start | bytes 393224 | tf_op jit(solution)/shard_map/ppermute | solution.py:19
  87.8 18.4 %collective-permute-start.5 = (f32[16,16,128]{2,1,0:T(8,128)S(1)}, f32[16,16,128]{2,1,0:T(8,128)S(1)}, u32[]{:S(2)}, u32[]{:S(2)}) collective-permute-start(f32[16,16,128]{2,1,0:T(8,128)S(1)} %fusion.293), channel_id=1, source_target_pairs={{4,0},{8,4},{12,8},{5,1},{9,5},{13,9},{6,2},{10,6},{14,10},{7,3},{... | collective-permute-start | bytes 393224 | tf_op jit(solution)/shard_map/ppermute | solution.py:22
  96.4 20.7 %collective-permute-start.10 = (f32[16,16,128]{2,1,0:T(8,128)S(1)}, f32[16,16,128]{2,1,0:T(8,128)S(1)}, u32[]{:S(2)}, u32[]{:S(2)}) collective-permute-start(f32[16,16,128]{2,1,0:T(8,128)S(1)} %fusion.262), channel_id=1, source_target_pairs={{0,4},{4,8},{8,12},{1,5},{5,9},{9,13},{2,6},{6,10},{10,14},{3,7},{... | collective-permute-start | bytes 393224 | tf_op jit(solution)/shard_map/ppermute | solution.py:19
  100.3 22.0 %collective-permute-start.11 = (f32[16,16,128]{2,1,0:T(8,128)S(1)}, f32[16,16,128]{2,1,0:T(8,128)S(1)}, u32[]{:S(2)}, u32[]{:S(2)}) collective-permute-start(f32[16,16,128]{2,1,0:T(8,128)S(1)} %fusion.262), channel_id=1, source_target_pairs={{4,0},{8,4},{12,8},{5,1},{9,5},{13,9},{6,2},{10,6},{14,10},{7,3},{... | collective-permute-start | bytes 393224 | tf_op jit(solution)/shard_map/ppermute | solution.py:22
  101.7 12.1 %collective-permute-start.32 = (f32[24,4,128]{2,1,0:T(4,128)S(1)}, f32[24,4,128]{2,1,0:T(4,128)S(1)}, u32[]{:S(2)}, u32[]{:S(2)}) collective-permute-start(f32[24,4,128]{2,1,0:T(4,128)S(1)} %get-tuple-element.24), channel_id=1, source_target_pairs={{2,0},{3,1},{6,4},{7,5},{10,8},{11,9},{14,12},{15,13},{18,16},{19,... | collective-permute-start | bytes 147464 | tf_op jit(solution)/shard_map/ppermute | solution.py:22
  103.0 12.1 %collective-permute-start.33 = (f32[24,4,128]{2,1,0:T(4,128)S(1)}, f32[24,4,128]{2,1,0:T(4,128)S(1)}, u32[]{:S(2)}, u32[]{:S(2)}) collective-permute-start(f32[24,4,128]{2,1,0:T(4,128)S(1)} %get-tuple-element.23), channel_id=1, source_target_pairs={{0,2},{1,3},{4,6},{5,7},{8,10},{9,11},{12,14},{13,15},{16,18},{17,... | collective-permute-start | bytes 147464 | tf_op jit(solution)/shard_map/ppermute | solution.py:19
  109.2 22.6 %collective-permute-start.16 = (f32[16,16,128]{2,1,0:T(8,128)S(1)}, f32[16,16,128]{2,1,0:T(8,128)S(1)}, u32[]{:S(2)}, u32[]{:S(2)}) collective-permute-start(f32[16,16,128]{2,1,0:T(8,128)S(1)} %fusion.231), channel_id=1, source_target_pairs={{0,4},{4,8},{8,12},{1,5},{5,9},{9,13},{2,6},{6,10},{10,14},{3,7},{... | collective-permute-start | bytes 393224 | tf_op jit(solution)/shard_map/ppermute | solution.py:19
  113.7 21.1 %collective-permute-start.17 = (f32[16,16,128]{2,1,0:T(8,128)S(1)}, f32[16,16,128]{2,1,0:T(8,128)S(1)}, u32[]{:S(2)}, u32[]{:S(2)}) collective-permute-start(f32[16,16,128]{2,1,0:T(8,128)S(1)} %fusion.231), channel_id=1, source_target_pairs={{4,0},{8,4},{12,8},{5,1},{9,5},{13,9},{6,2},{10,6},{14,10},{7,3},{... | collective-permute-start | bytes 393224 | tf_op jit(solution)/shard_map/ppermute | solution.py:22
  115.8 13.3 %collective-permute-start.36 = (f32[4,16,128]{2,1,0:T(8,128)S(1)}, f32[4,16,128]{2,1,0:T(8,128)S(1)}, u32[]{:S(2)}, u32[]{:S(2)}) collective-permute-start(f32[4,16,128]{2,1,0:T(8,128)S(1)} %get-tuple-element.47), channel_id=1, source_target_pairs={{4,0},{8,4},{12,8},{5,1},{9,5},{13,9},{6,2},{10,6},{14,10},{7,3},{... | collective-permute-start | bytes 98312 | tf_op jit(solution)/shard_map/ppermute | solution.py:22
  117.1 13.3 %collective-permute-start.37 = (f32[4,16,128]{2,1,0:T(8,128)S(1)}, f32[4,16,128]{2,1,0:T(8,128)S(1)}, u32[]{:S(2)}, u32[]{:S(2)}) collective-permute-start(f32[4,16,128]{2,1,0:T(8,128)S(1)} %get-tuple-element.48), channel_id=1, source_target_pairs={{0,4},{4,8},{8,12},{1,5},{5,9},{9,13},{2,6},{6,10},{10,14},{3,7},{... | collective-permute-start | bytes 98312 | tf_op jit(solution)/shard_map/ppermute | solution.py:19
  125.2 20.4 %collective-permute-start.22 = (f32[16,16,128]{2,1,0:T(8,128)S(1)}, f32[16,16,128]{2,1,0:T(8,128)S(1)}, u32[]{:S(2)}, u32[]{:S(2)}) collective-permute-start(f32[16,16,128]{2,1,0:T(8,128)S(1)} %fusion.200), channel_id=1, source_target_pairs={{0,4},{4,8},{8,12},{1,5},{5,9},{9,13},{2,6},{6,10},{10,14},{3,7},{... | collective-permute-start | bytes 393224 | tf_op jit(solution)/shard_map/ppermute | solution.py:19
  129.1 21.7 %collective-permute-start.23 = (f32[16,16,128]{2,1,0:T(8,128)S(1)}, f32[16,16,128]{2,1,0:T(8,128)S(1)}, u32[]{:S(2)}, u32[]{:S(2)}) collective-permute-start(f32[16,16,128]{2,1,0:T(8,128)S(1)} %fusion.200), channel_id=1, source_target_pairs={{4,0},{8,4},{12,8},{5,1},{9,5},{13,9},{6,2},{10,6},{14,10},{7,3},{... | collective-permute-start | bytes 393224 | tf_op jit(solution)/shard_map/ppermute | solution.py:22
  130.5 11.8 %collective-permute-start.38 = (f32[24,4,128]{2,1,0:T(4,128)S(1)}, f32[24,4,128]{2,1,0:T(4,128)S(1)}, u32[]{:S(2)}, u32[]{:S(2)}) collective-permute-start(f32[24,4,128]{2,1,0:T(4,128)S(1)} %get-tuple-element.20), channel_id=1, source_target_pairs={{2,0},{3,1},{6,4},{7,5},{10,8},{11,9},{14,12},{15,13},{18,16},{19,... | collective-permute-start | bytes 147464 | tf_op jit(solution)/shard_map/ppermute | solution.py:22
  131.8 11.8 %collective-permute-start.39 = (f32[24,4,128]{2,1,0:T(4,128)S(1)}, f32[24,4,128]{2,1,0:T(4,128)S(1)}, u32[]{:S(2)}, u32[]{:S(2)}) collective-permute-start(f32[24,4,128]{2,1,0:T(4,128)S(1)} %get-tuple-element.19), channel_id=1, source_target_pairs={{0,2},{1,3},{4,6},{5,7},{8,10},{9,11},{12,14},{13,15},{16,18},{17,... | collective-permute-start | bytes 147464 | tf_op jit(solution)/shard_map/ppermute | solution.py:19
  137.7 22.5 %collective-permute-start.28 = (f32[16,16,128]{2,1,0:T(8,128)S(1)}, f32[16,16,128]{2,1,0:T(8,128)S(1)}, u32[]{:S(2)}, u32[]{:S(2)}) collective-permute-start(f32[16,16,128]{2,1,0:T(8,128)S(1)} %fusion.169), channel_id=1, source_target_pairs={{0,4},{4,8},{8,12},{1,5},{5,9},{9,13},{2,6},{6,10},{10,14},{3,7},{... | collective-permute-start | bytes 393224 | tf_op jit(solution)/shard_map/ppermute | solution.py:19
  142.2 21.0 %collective-permute-start.29 = (f32[16,16,128]{2,1,0:T(8,128)S(1)}, f32[16,16,128]{2,1,0:T(8,128)S(1)}, u32[]{:S(2)}, u32[]{:S(2)}) collective-permute-start(f32[16,16,128]{2,1,0:T(8,128)S(1)} %fusion.169), channel_id=1, source_target_pairs={{4,0},{8,4},{12,8},{5,1},{9,5},{13,9},{6,2},{10,6},{14,10},{7,3},{... | collective-permute-start | bytes 393224 | tf_op jit(solution)/shard_map/ppermute | solution.py:22
  144.3 13.2 %collective-permute-start.42 = (f32[4,16,128]{2,1,0:T(8,128)S(1)}, f32[4,16,128]{2,1,0:T(8,128)S(1)}, u32[]{:S(2)}, u32[]{:S(2)}) collective-permute-start(f32[4,16,128]{2,1,0:T(8,128)S(1)} %get-tuple-element.45), channel_id=1, source_target_pairs={{4,0},{8,4},{12,8},{5,1},{9,5},{13,9},{6,2},{10,6},{14,10},{7,3},{... | collective-permute-start | bytes 98312 | tf_op jit(solution)/shard_map/ppermute | solution.py:22
  145.6 13.2 %collective-permute-start.43 = (f32[4,16,128]{2,1,0:T(8,128)S(1)}, f32[4,16,128]{2,1,0:T(8,128)S(1)}, u32[]{:S(2)}, u32[]{:S(2)}) collective-permute-start(f32[4,16,128]{2,1,0:T(8,128)S(1)} %get-tuple-element.46), channel_id=1, source_target_pairs={{0,4},{4,8},{8,12},{1,5},{5,9},{9,13},{2,6},{6,10},{10,14},{3,7},{... | collective-permute-start | bytes 98312 | tf_op jit(solution)/shard_map/ppermute | solution.py:19
  153.6 23.8 %collective-permute-start.34 = (f32[16,16,128]{2,1,0:T(8,128)S(1)}, f32[16,16,128]{2,1,0:T(8,128)S(1)}, u32[]{:S(2)}, u32[]{:S(2)}) collective-permute-start(f32[16,16,128]{2,1,0:T(8,128)S(1)} %fusion.138), channel_id=1, source_target_pairs={{0,4},{4,8},{8,12},{1,5},{5,9},{9,13},{2,6},{6,10},{10,14},{3,7},{... | collective-permute-start | bytes 393224 | tf_op jit(solution)/shard_map/ppermute | solution.py:19
  157.6 21.2 %collective-permute-start.35 = (f32[16,16,128]{2,1,0:T(8,128)S(1)}, f32[16,16,128]{2,1,0:T(8,128)S(1)}, u32[]{:S(2)}, u32[]{:S(2)}) collective-permute-start(f32[16,16,128]{2,1,0:T(8,128)S(1)} %fusion.138), channel_id=1, source_target_pairs={{4,0},{8,4},{12,8},{5,1},{9,5},{13,9},{6,2},{10,6},{14,10},{7,3},{... | collective-permute-start | bytes 393224 | tf_op jit(solution)/shard_map/ppermute | solution.py:22
  158.9 11.9 %collective-permute-start.44 = (f32[24,4,128]{2,1,0:T(4,128)S(1)}, f32[24,4,128]{2,1,0:T(4,128)S(1)}, u32[]{:S(2)}, u32[]{:S(2)}) collective-permute-start(f32[24,4,128]{2,1,0:T(4,128)S(1)} %get-tuple-element.16), channel_id=1, source_target_pairs={{2,0},{3,1},{6,4},{7,5},{10,8},{11,9},{14,12},{15,13},{18,16},{19,... | collective-permute-start | bytes 147464 | tf_op jit(solution)/shard_map/ppermute | solution.py:22
  160.2 11.9 %collective-permute-start.45 = (f32[24,4,128]{2,1,0:T(4,128)S(1)}, f32[24,4,128]{2,1,0:T(4,128)S(1)}, u32[]{:S(2)}, u32[]{:S(2)}) collective-permute-start(f32[24,4,128]{2,1,0:T(4,128)S(1)} %get-tuple-element.15), channel_id=1, source_target_pairs={{0,2},{1,3},{4,6},{5,7},{8,10},{9,11},{12,14},{13,15},{16,18},{17,... | collective-permute-start | bytes 147464 | tf_op jit(solution)/shard_map/ppermute | solution.py:19
  166.2 15.4 %collective-permute-start.40 = (f32[16,16,128]{2,1,0:T(8,128)S(1)}, f32[16,16,128]{2,1,0:T(8,128)S(1)}, u32[]{:S(2)}, u32[]{:S(2)}) collective-permute-start(f32[16,16,128]{2,1,0:T(8,128)S(1)} %fusion.107), channel_id=1, source_target_pairs={{0,4},{4,8},{8,12},{1,5},{5,9},{9,13},{2,6},{6,10},{10,14},{3,7},{... | collective-permute-start | bytes 393224 | tf_op jit(solution)/shard_map/ppermute | solution.py:19
  (31 other events, 337.6 us)
Sparse Core Ops, SparseCore 0:
  202.4 56.4 reduce-scatter.1
where the time goes:
time: 270 us; the launch traced here: 269 us
  starting transfers between devices  130 us (48%)
  waiting for transfers between devices  60.6 us (22%)
  other arithmetic  29.2 us (11%)
  local copies, waits for them, and re-layouts  24.7 us (9%)
  between operations  15.8 us (6%)
  matrix products  8.84 us (3%)
    ppermute x24, starting transfers between devices, with_halo(): lax.ppermute(lax.slice_in_dim(block, block.shape[dim] - width, None, axis...  98.8 us
    reduce_scatter x1, waiting for transfers between devices, on_device(): lax.psum_scatter(accumulated, 'shot', scatter_dimension=0, tiled=True)  56.5 us
    ppermute x24, starting transfers between devices, with_halo(): lax.ppermute(lax.slice_in_dim(block, 0, width, axis=dim), axis, backward)  31 us
    gather x8, local copies, waits for them, and re-layouts, one_lag(): return lax.dynamic_slice_in_dim(lag_view, offset + lag_reach, cell_rows, 0)  22.7 us
    add x1, other arithmetic, on_device(): accumulated = accumulated + source[None] * jax.vmap(one_lag)(lag_list)  15 us
    dot_general x8, matrix products, on_device(): jnp.dot(weighted.T, hit_cols, precision=lax.Precision.HIGHEST, preferred_...  8.84 us
    concatenate x32, other arithmetic, with_halo(): block = jnp.concatenate([low, block, high], axis=dim)  6.15 us
  transfers between devices with their start and end apart: 49, of which 6 were waited for; matrix products, arithmetic and copies ran while one was open for 12% of the time, Pallas kernels for 0%

commit v1 on v0

v1 whole, which is shorter than its diff:
```python
import functools

import jax
import jax.numpy as jnp
from jax import lax
from jax.experimental import pallas as pl
from jax.experimental.pallas import tpu as pltpu
from jax.sharding import PartitionSpec as P

NLAG = 32
REACH = NLAG // 2
SIDE = 8

stencil_weights = (-205.0 / 72.0, 8.0 / 5.0, -1.0 / 5.0, 8.0 / 315.0, -1.0 / 560.0)
mute_reach = 3
receiver_depth = 1
MESH = pl.DeviceIdType.MESH


def kernel(
    sizes,
    lags,
    src_at_inline,
    src_at_xline,
    vel2,
    adj_prev,
    adj_now,
    residual,
    rec_inline,
    rec_xline,
    src_field,
    out,
    *scratch,
):
    shots, n_inline, n_xline, rows, cols, depth, steps = sizes
    fields = [
        [scratch[s * (steps + 1) + t] for t in range(steps + 1)] for s in range(shots)
    ]
    (older0, src, surf, surf_send, surf_recv, load_sem, prev_send, prev_recv, now_send, now_recv,
     src_send, src_recv, z_send, z_recv, j_send, j_recv) = scratch[shots * (steps + 1):]
    me_shot = lax.axis_index("shot")
    me_in = lax.axis_index("inline")
    me_x = lax.axis_index("xline")
    has_low, has_high = me_in > 0, me_in < n_inline - 1
    has_left, has_right = me_x > 0, me_x < n_xline - 1
    tile_rows = pl.ds(REACH, rows)
    tile_cols = pl.ds(SIDE, cols)

    def partner(d):
        return {"shot": lax.rem(me_shot + d, shots)}

    barrier = pltpu.get_barrier_semaphore()

    def greet(where):
        pl.semaphore_signal(barrier, inc=1, device_id=where, device_id_type=MESH)

    @pl.when(has_low)
    def _():
        greet({"inline": me_in - 1})

    @pl.when(has_high)
    def _():
        greet({"inline": me_in + 1})

    @pl.when(has_left)
    def _():
        greet({"xline": me_x - 1})

    @pl.when(has_right)
    def _():
        greet({"xline": me_x + 1})

    for d in range(1, shots):
        greet(partner(d))

    load_src = pltpu.make_async_copy(src_field.at[0], src.at[0], load_sem)
    load_src.start()
    fields[0][0][tile_rows, tile_cols, :] = adj_now[0]
    older0[0] = adj_prev[0]

    near = 4

    def z_copy(s, t, which, here, there, count, step_to):
        ref = fields[s][t]
        return pltpu.make_async_remote_copy(
            src_ref=ref.at[pl.ds(here, count), tile_cols, :],
            dst_ref=ref.at[pl.ds(there, count), tile_cols, :],
            send_sem=z_send.at[s, t, which],
            recv_sem=z_recv.at[s, t, which],
            device_id={"inline": me_in + step_to},
            device_id_type=MESH,
        )

    def z_near(s, t):
        return [
            (has_low, has_high, z_copy(s, t, 0, REACH, REACH + rows, near, -1)),
            (has_high, has_low, z_copy(s, t, 1, REACH + rows - near, REACH - near, near, 1)),
        ]

    def z_far(s, t):
        return [
            (has_low, has_high,
             z_copy(s, t, 2, REACH + near, REACH + rows + near, rows - near, -1)),
            (has_high, has_low, z_copy(s, t, 3, REACH, REACH - rows, rows - near, 1)),
        ]

    def j_side(s, t):
        ref = fields[s][t]
        left = pltpu.make_async_remote_copy(
            src_ref=ref.at[tile_rows, pl.ds(SIDE, SIDE), :],
            dst_ref=ref.at[tile_rows, pl.ds(SIDE + cols, SIDE), :],
            send_sem=j_send.at[s, t, 0],
            recv_sem=j_recv.at[s, t, 0],
            device_id={"xline": me_x - 1},
            device_id_type=MESH,
        )
        right = pltpu.make_async_remote_copy(
            src_ref=ref.at[tile_rows, pl.ds(cols, SIDE), :],
            dst_ref=ref.at[tile_rows, pl.ds(0, SIDE), :],
            send_sem=j_send.at[s, t, 1],
            recv_sem=j_recv.at[s, t, 1],
            device_id={"xline": me_x + 1},
            device_id_type=MESH,
        )
        return [(has_left, has_right, left), (has_right, has_left, right)]

    started = []

    def start(copies):
        for sends, _, copy in copies:
            pl.when(sends)(copy.start)
        started.extend(copies)

    def await_recv(copies):
        for _, receives, copy in copies:
            pl.when(receives)(copy.wait_recv)

    pl.semaphore_wait(
        barrier,
        has_low.astype(jnp.int32) + has_high.astype(jnp.int32)
        + has_left.astype(jnp.int32) + has_right.astype(jnp.int32) + (shots - 1),
    )

    start(z_near(0, 0))
    start(j_side(0, 0))

    def to_shot(d, src_ref, dst_ref, send_sem, recv_sem):
        return pltpu.make_async_remote_copy(
            src_ref=src_ref, dst_ref=dst_ref, send_sem=send_sem, recv_sem=recv_sem,
            device_id=partner(d), device_id_type=MESH,
        )

    shot_copies = []

    def now_copy(d):
        return to_shot(
            d, fields[0][0].at[tile_rows, tile_cols, :],
            fields[shots - d][0].at[tile_rows, tile_cols, :],
            now_send.at[d], now_recv.at[shots - d])

    def prev_copy(d):
        return to_shot(d, older0.at[0], older0.at[shots - d], prev_send.at[d],
                       prev_recv.at[shots - d])

    def surf_copy(d):
        return to_shot(d, surf.at[0], surf.at[shots - d], surf_send.at[d],
                       surf_recv.at[shots - d])

    def src_copy(d, t):
        return to_shot(d, src.at[0, t], src.at[shots - d, t], src_send.at[d, t],
                       src_recv.at[shots - d, t])

    def start_shot(copy):
        copy.start()
        shot_copies.append(copy)

    for d in range(1, shots):
        start_shot(now_copy(d))
    for d in range(1, shots):
        start_shot(prev_copy(d))

    row_ids = me_in * rows + lax.broadcasted_iota(jnp.int32, (rows, 1), 0)
    col_ids = me_x * cols + lax.broadcasted_iota(jnp.int32, (cols, 1), 0)
    hit_rows = (rec_inline[...] == row_ids).astype(jnp.float32)
    hit_cols = (rec_xline[...] == col_ids).astype(jnp.float32)
    weighted = jnp.concatenate(
        [hit_rows * residual[0, t : t + 1, :] for t in range(steps)], axis=0
    )
    surf[0] = lax.dot_general(
        hit_cols, weighted, (((1,), (1,)), ((), ())),
        precision=lax.Precision.HIGHEST, preferred_element_type=jnp.float32,
    )
    for d in range(1, shots):
        start_shot(surf_copy(d))

    @pl.when(jnp.logical_not(has_low))
    def _():
        for s in range(shots):
            for t in range(steps + 1):
                fields[s][t][0:REACH, tile_cols, :] = jnp.zeros((REACH, cols, depth), jnp.float32)

    @pl.when(jnp.logical_not(has_high))
    def _():
        for s in range(shots):
            for t in range(steps + 1):
                fields[s][t][pl.ds(REACH + rows, REACH), tile_cols, :] = jnp.zeros(
                    (REACH, cols, depth), jnp.float32)

    @pl.when(jnp.logical_not(has_left))
    def _():
        for s in range(shots):
            for t in range(steps):
                fields[s][t][tile_rows, 0:SIDE, :] = jnp.zeros((rows, SIDE, depth), jnp.float32)

    @pl.when(jnp.logical_not(has_right))
    def _():
        for s in range(shots):
            for t in range(steps):
                fields[s][t][tile_rows, pl.ds(SIDE + cols, SIDE), :] = jnp.zeros(
                    (rows, SIDE, depth), jnp.float32)

    load_src.wait()
    at_inline, at_xline = src_at_inline[0], src_at_xline[0]
    cell_cols = me_x * cols + lax.broadcasted_iota(jnp.int32, (cols, depth), 0)
    col_inside = (jnp.abs(cell_cols - at_xline) <= mute_reach).astype(jnp.float32)
    for t in range(steps):
        def mute_row(i, carry):
            hit = (jnp.abs(me_in * rows + i - at_inline) <= mute_reach).astype(jnp.float32)
            src[0, t, i] = src[0, t, i] * (1.0 - hit * col_inside)
            return carry

        lax.fori_loop(0, rows, mute_row, 0)
        for d in range(1, shots):
            start_shot(src_copy(d, t))

    lanes = lax.broadcasted_iota(jnp.int32, (cols, depth), 1)

    def advance(s, t):
        now, new = fields[s][t], fields[s][t + 1]

        def one_row(i):
            at = REACH + i
            centre = now[at, tile_cols, :]
            total = 3.0 * stencil_weights[0] * centre
            for reach in range(1, 5):
                up = jnp.where(lanes >= reach, pltpu.roll(centre, reach, 1), 0.0)
                down = jnp.where(
                    lanes < depth - reach, pltpu.roll(centre, depth - reach, 1), 0.0)
                total = total + stencil_weights[reach] * (
                    (now[at + reach, tile_cols, :] + now[at - reach, tile_cols, :])
                    + (now[at, pl.ds(SIDE + reach, cols), :]
                       + now[at, pl.ds(SIDE - reach, cols), :])
                    + (up + down))
            shift = lax.rem(receiver_depth - (t * rows + i) + 2 * depth, depth)
            injected = jnp.where(
                lanes == receiver_depth, pltpu.roll(surf[s], shift, 1), 0.0)
            before = older0[s, i] if t == 0 else fields[s][t - 1][at, tile_cols, :]
            new[at, tile_cols, :] = 2.0 * centre - before + vel2[i] * (total + injected)

        def some_rows(b, carry):
            for i in range(4):
                one_row(b * 4 + i)
            return carry

        lax.fori_loop(0, rows // 4, some_rows, 0)

    own_count = NLAG // shots
    first_lag = me_shot * own_count

    def correlate(t):
        last = t == steps

        def one_row(i, carry):
            sources = [src[s, t - 1, i] for s in range(shots)]
            for k in range(own_count):
                lag = lags[first_lag + k]
                at = REACH + i + lag
                total = sources[0] * fields[0][t][at, tile_cols, :]
                for s in range(1, shots):
                    total = total + sources[s] * fields[s][t][at, tile_cols, :]
                if t > 1:
                    total = out[k, i] + total
                if last:
                    total = total * jnp.abs(lag).astype(jnp.float32)
                out[k, i] = total
            return carry

        lax.fori_loop(0, rows, one_row, 0)

    for t in range(steps):
        for s in range(shots):
            if t == 0 and s > 0:
                now_copy(shots - s).wait_recv()
                start(z_near(s, 0))
                start(j_side(s, 0))
        for s in range(shots):
            if t == 0 and s > 0:
                prev_copy(shots - s).wait_recv()
                surf_copy(shots - s).wait_recv()
            await_recv(j_side(s, t))
            await_recv(z_near(s, t))
            advance(s, t)
            start(z_near(s, t + 1))
            if t + 1 < steps:
                start(j_side(s, t + 1))
            start(z_far(s, t + 1))
        if t > 0:
            for s in range(shots):
                await_recv(z_far(s, t))
                if s > 0:
                    src_copy(shots - s, t - 1).wait_recv()
            correlate(t)
    for s in range(shots):
        await_recv(z_near(s, steps))
        await_recv(z_far(s, steps))
        if s > 0:
            src_copy(shots - s, steps - 1).wait_recv()
    correlate(steps)

    for sends, _, copy in started:
        pl.when(sends)(copy.wait_send)
    for copy in shot_copies:
        copy.wait_send()


def on_device(
    sizes,
    vel2,
    adj_prev,
    adj_now,
    src_field,
    residual,
    rec_inline,
    rec_xline,
    src_inline,
    src_xline,
    lag_list,
):
    shots, _, _, rows, cols, depth, steps = sizes
    vmem = pl.BlockSpec(memory_space=pltpu.VMEM)
    smem = pl.BlockSpec(memory_space=pltpu.SMEM)
    field = pltpu.VMEM((rows + 2 * REACH, cols + 2 * SIDE, depth), jnp.float32)
    dma = pltpu.SemaphoreType.DMA
    return pl.pallas_call(
        functools.partial(kernel, sizes),
        out_shape=jax.ShapeDtypeStruct((NLAG // shots, rows, cols, depth), jnp.float32),
        in_specs=[smem, smem, smem, vmem, vmem, vmem, vmem, vmem, vmem,
                  pl.BlockSpec(memory_space=pl.ANY)],
        out_specs=vmem,
        scratch_shapes=[field] * (shots * (steps + 1)) + [
            pltpu.VMEM((shots, rows, cols, depth), jnp.float32),
            pltpu.VMEM((shots, steps, rows, cols, depth), jnp.float32),
            pltpu.VMEM((shots, cols, depth), jnp.float32),
            dma((shots,)), dma((shots,)),
            dma,
            dma((shots,)), dma((shots,)),
            dma((shots,)), dma((shots,)),
            dma((shots, steps)), dma((shots, steps)),
            dma((shots, steps + 1, 4)), dma((shots, steps + 1, 4)),
            dma((shots, steps + 1, 2)), dma((shots, steps + 1, 2)),
        ],
        compiler_params=pltpu.CompilerParams(
            collective_id=0, has_side_effects=True, vmem_limit_bytes=52 * 2**20),
        name="adjoint_window",
    )(lag_list, src_inline, src_xline, vel2, adj_prev, adj_now, residual, rec_inline, rec_xline,
      src_field)


def solution(mesh):
    in_specs = (
        P("inline", "xline", None),
        P(("group", "shot"), "inline", "xline", None),
        P(("group", "shot"), "inline", "xline", None),
        P(("group", "shot"), None, "inline", "xline", None),
        P(("group", "shot"), None, None),
        P(("group", "shot"), None),
        P(("group", "shot"), None),
        P(("group", "shot")),
        P(("group", "shot")),
        P(),
    )
    out_specs = P(("group", "shot"), "inline", "xline", None)

    def whole(vel2, adj_prev, adj_now, src_field, *rest):
        n_inline, n_xline = mesh.shape["inline"], mesh.shape["xline"]
        sizes = (mesh.shape["shot"], n_inline, n_xline, vel2.shape[0] // n_inline,
                 vel2.shape[1] // n_xline, vel2.shape[2], src_field.shape[1])
        return jax.shard_map(
            functools.partial(on_device, sizes), mesh=mesh, in_specs=in_specs,
            out_specs=out_specs, check_vma=False,
        )(vel2, adj_prev, adj_now, src_field, *rest)

    return whole
```

time: 270 us -> 72.8 us (0.27)
  starting transfers between devices: 130 us -> 0 us
  Pallas kernels: 0 us -> 61.3 us
  waiting for transfers between devices: 60.6 us -> 0 us
  other arithmetic: 29.2 us -> 0 us
  local copies, waits for them, and re-layouts: 24.7 us -> 9.81 us
  between operations: 15.8 us -> 1.32 us
  matrix products: 8.84 us -> 0 us
    ppermute x48 -> x0, starting transfers between devices: 130 us -> none  [the longest x24 98.8 us: with_halo(): lax.ppermute(lax.slice_in_dim(block, block.shape[dim] - width, None, axis...]
    pallas_call x0 -> x1, Pallas kernels: none -> 61.3 us  [on_device(): pl.pallas_call(functools.partial(kernel, sizes), out_shape=jax.ShapeDtype...]
    reduce_scatter x1 -> x0, waiting for transfers between devices: 56.5 us -> none  [on_device(): lax.psum_scatter(accumulated, 'shot', scatter_dimension=0, tiled=True)]
    gather x8 -> x0, local copies, waits for them, and re-layouts: 22.7 us -> none  [one_lag(): return lax.dynamic_slice_in_dim(lag_view, offset + lag_reach, cell_rows, 0)]
    add x10 -> x0, other arithmetic: 19.5 us -> none  [the longest x1 15 us: on_device(): accumulated = accumulated + source[None] * jax.vmap(one_lag)(lag_list)]
    unnamed x12 -> x17, local copies, waits for them, and re-layouts: 0.03 us -> 9.81 us
    dot_general x8 -> x0, matrix products: 8.84 us -> none  [on_device(): jnp.dot(weighted.T, hit_cols, precision=lax.Precision.HIGHEST, preferred_...]
    concatenate x33 -> x0, other arithmetic: 6.15 us -> none  [the longest x32 6.15 us: with_halo(): block = jnp.concatenate([low, block, high], axis=dim)]
  transfers between devices with their start and end apart: 49 -> 0, of which waited for: 6 -> 0; matrix products, arithmetic and copies ran while one was open for 12% -> 0% of each run, Pallas kernels for 0% -> 0%
where the time goes in v1:
time: 72.8 us; the launch traced here: 72.5 us
  Pallas kernels  61.3 us (84%)
  local copies, waits for them, and re-layouts  9.81 us (13%)
  between operations  1.32 us (2%)
    pallas_call x1, Pallas kernels, on_device(): pl.pallas_call(functools.partial(kernel, sizes), out_shape=jax.ShapeDtype...  61.3 us
    unnamed x17, local copies, waits for them, and re-layouts  9.81 us

profile of v1, /device:TPU:0, one launch (start us, length us, event | category | flops | bytes accessed | tf_op | source)
XLA Modules:
  0.0 72.5 jit_solution(1144530195294852742)
XLA Ops:
  1.3 0.0 copy-start
  1.3 1.2 %copy-done = f32[1,8,16,16,128]{4,3,2,1,0:T(8,128)S(1)} copy-done((f32[1,8,16,16,128]{4,3,2,1,0:T(8,128)S(1)}, f32[1,8,16,16,128]{4,3,2,1,0:T(8,128)}, u32[]{:S(2)}) %copy-start) | copy-done | bytes 1048600
  2.5 0.0 copy-start.1
  2.5 0.9 %copy-done.1 = f32[16,16,128]{2,1,0:T(8,128)S(1)} copy-done((f32[16,16,128]{2,1,0:T(8,128)S(1)}, f32[16,16,128]{2,1,0:T(8,128)}, u32[]{:S(2)}) %copy-start.1) | copy-done | bytes 131096
  3.4 0.0 copy-start.2
  3.4 0.9 %copy-done.2 = f32[1,16,16,128]{3,2,1,0:T(8,128)S(1)} copy-done((f32[1,16,16,128]{3,2,1,0:T(8,128)S(1)}, f32[1,16,16,128]{3,2,1,0:T(8,128)}, u32[]{:S(2)}) %copy-start.2) | copy-done | bytes 131096
  4.3 0.0 copy-start.3
  4.3 0.9 %copy-done.3 = f32[1,16,16,128]{3,2,1,0:T(8,128)S(1)} copy-done((f32[1,16,16,128]{3,2,1,0:T(8,128)S(1)}, f32[1,16,16,128]{3,2,1,0:T(8,128)}, u32[]{:S(2)}) %copy-start.3) | copy-done | bytes 131096
  5.2 0.0 copy-start.4
  5.2 0.8 %copy-done.4 = f32[1,8,1024]{2,1,0:T(8,128)S(1)} copy-done((f32[1,8,1024]{2,1,0:T(8,128)S(1)}, f32[1,8,1024]{2,1,0:T(8,128)}, u32[]{:S(2)}) %copy-start.4) | copy-done | bytes 32792
  6.0 0.0 copy-start.5
  6.0 0.7 copy-done.5
  6.7 0.0 copy-start.6
  6.7 0.7 copy-done.6
  7.4 0.0 copy-start.7
  7.4 0.7 copy-done.7
  8.0 61.3 %adjoint_window.1 = f32[16,16,16,128]{3,2,1,0:T(8,128)} custom-call(s32[32]{0:T(128)S(1)} %copy-done.7, s32[1]{0:T(128)S(6)} %copy.12.src_at_inline, s32[1]{0:T(128)S(6)} %copy.13.src_at_xline, f32[16,16,128]{2,1,0:T(8,128)S(1)} %copy-done.1, f32[1,16,16,128]{3,2,1,0:T(8,128)S(1)} %copy-done.2, f32[1,16,16,128]{3,2,1,0:T(8,128)S(1)} %copy-done.3, ...), custom_call_target="tpu_custom_call" | custom-call | tf_op jit(solution)/shard_map/adjoint_window/pallas_call | solution.py:344
  69.4 3.1 %copy.14 = f32[16,16,16,128]{3,2,1,0:T(8,128)} copy(f32[16,16,16,128]{3,2,1,0:T(8,128)} %adjoint_window.1) | data formatting | bytes 4194304
Async XLA Ops:
  1.3 1.2 %copy-start = (f32[1,8,16,16,128]{4,3,2,1,0:T(8,128)S(1)}, f32[1,8,16,16,128]{4,3,2,1,0:T(8,128)}, u32[]{:S(2)}) copy-start(f32[1,8,16,16,128]{4,3,2,1,0:T(8,128)} %src_field.1) | copy-start | bytes 3145732
  2.5 0.9 %copy-start.1 = (f32[16,16,128]{2,1,0:T(8,128)S(1)}, f32[16,16,128]{2,1,0:T(8,128)}, u32[]{:S(2)}) copy-start(f32[16,16,128]{2,1,0:T(8,128)} %vel2.1) | copy-start | bytes 393220
  3.4 0.9 %copy-start.2 = (f32[1,16,16,128]{3,2,1,0:T(8,128)S(1)}, f32[1,16,16,128]{3,2,1,0:T(8,128)}, u32[]{:S(2)}) copy-start(f32[1,16,16,128]{3,2,1,0:T(8,128)} %adj_prev.1) | copy-start | bytes 393220
  4.3 0.9 %copy-start.3 = (f32[1,16,16,128]{3,2,1,0:T(8,128)S(1)}, f32[1,16,16,128]{3,2,1,0:T(8,128)}, u32[]{:S(2)}) copy-start(f32[1,16,16,128]{3,2,1,0:T(8,128)} %adj_now.1) | copy-start | bytes 393220
  5.2 0.8 %copy-start.4 = (f32[1,8,1024]{2,1,0:T(8,128)S(1)}, f32[1,8,1024]{2,1,0:T(8,128)}, u32[]{:S(2)}) copy-start(f32[1,8,1024]{2,1,0:T(8,128)} %residual.1) | copy-start | bytes 98308
  6.0 0.7 copy-start.5
  6.7 0.7 copy-start.6
  7.4 0.7 copy-start.7

commit v2 on v1

v2 whole, which is shorter than its diff:
```python
import functools

import jax
import jax.numpy as jnp
from jax import lax
from jax.experimental import pallas as pl
from jax.experimental.pallas import tpu as pltpu
from jax.sharding import PartitionSpec as P

NLAG = 32
REACH = NLAG // 2
NEAR = 4
EXTRA = REACH - NEAR
SIDE = 8

stencil_weights = (-205.0 / 72.0, 8.0 / 5.0, -1.0 / 5.0, 8.0 / 315.0, -1.0 / 560.0)
mute_reach = 3
receiver_depth = 1
MESH = pl.DeviceIdType.MESH


def kernel(
    sizes,
    lags_in,
    src_at_inline_in,
    src_at_xline_in,
    vel2_in,
    adj_prev_in,
    adj_now_in,
    residual_in,
    rec_inline_in,
    rec_xline_in,
    src_field,
    out,
    *scratch,
):
    shots, n_inline, n_xline, rows, cols, depth, steps = sizes
    fields = [
        [scratch[s * (steps + 1) + t] for t in range(steps + 1)] for s in range(shots)
    ]
    (lags, src_at_inline, src_at_xline, vel2, older0, residual, rec_inline, rec_xline,
     src, surf, load_sem, vel_send, vel_recv, surf_send, surf_recv, now_send, now_recv,
     src_send, src_recv, z_send, z_recv, j_send, j_recv) = scratch[shots * (steps + 1):]
    me_shot = lax.axis_index("shot")
    me_in = lax.axis_index("inline")
    me_x = lax.axis_index("xline")
    has_low, has_high = me_in > 0, me_in < n_inline - 1
    has_left, has_right = me_x > 0, me_x < n_xline - 1
    tile_rows = pl.ds(REACH, rows)
    tile_cols = pl.ds(SIDE, cols)

    loads = [
        pltpu.make_async_copy(src_ref, dst_ref, load_sem.at[n])
        for n, (src_ref, dst_ref) in enumerate([
            (adj_now_in.at[0], fields[0][0].at[tile_rows, tile_cols, :]),
            (adj_prev_in.at[0], older0),
            (vel2_in, vel2.at[tile_rows]),
            (residual_in.at[0], residual),
            (rec_inline_in, rec_inline),
            (rec_xline_in, rec_xline),
            (src_field.at[0], src.at[0]),
            (lags_in, lags),
            (src_at_inline_in, src_at_inline),
            (src_at_xline_in, src_at_xline),
        ])
    ]
    for load in loads:
        load.start()

    def partner(d):
        return {"shot": lax.rem(me_shot + d, shots)}

    barrier = pltpu.get_barrier_semaphore()

    def greet(where):
        pl.semaphore_signal(barrier, inc=1, device_id=where, device_id_type=MESH)

    @pl.when(has_low)
    def _():
        greet({"inline": me_in - 1})

    @pl.when(has_high)
    def _():
        greet({"inline": me_in + 1})

    @pl.when(has_left)
    def _():
        greet({"xline": me_x - 1})

    @pl.when(has_right)
    def _():
        greet({"xline": me_x + 1})

    for d in range(1, shots):
        greet(partner(d))

    def z_copy(s, t, which, here, there, count, step_to):
        ref = fields[s][t]
        return pltpu.make_async_remote_copy(
            src_ref=ref.at[pl.ds(here, count), tile_cols, :],
            dst_ref=ref.at[pl.ds(there, count), tile_cols, :],
            send_sem=z_send.at[s, t, which],
            recv_sem=z_recv.at[s, t, which],
            device_id={"inline": me_in + step_to},
            device_id_type=MESH,
        )

    def z_rows(s, t, which, begin, end):
        return [
            (has_low, has_high,
             z_copy(s, t, which, REACH + begin, REACH + rows + begin, end - begin, -1)),
            (has_high, has_low,
             z_copy(s, t, which + 1, REACH + rows - end, REACH - end, end - begin, 1)),
        ]

    def z_near(s, t):
        if t >= 3:
            return z_rows(s, t, 0, EXTRA, REACH)
        return z_rows(s, t, 0, 0, NEAR)

    def z_far(s, t):
        return z_rows(s, t, 2, NEAR, REACH)

    def z_vel():
        def one(which, here, there, step_to):
            return pltpu.make_async_remote_copy(
                src_ref=vel2.at[pl.ds(here, EXTRA)], dst_ref=vel2.at[pl.ds(there, EXTRA)],
                send_sem=vel_send.at[which], recv_sem=vel_recv.at[which],
                device_id={"inline": me_in + step_to}, device_id_type=MESH)

        return [(has_low, has_high, one(0, REACH, REACH + rows, -1)),
                (has_high, has_low, one(1, REACH + rows - EXTRA, REACH - EXTRA, 1))]

    def j_copy(s, t, which, begin, count):
        ref = fields[s][t]
        some_rows = pl.ds(begin, count)
        left = pltpu.make_async_remote_copy(
            src_ref=ref.at[some_rows, pl.ds(SIDE, SIDE), :],
            dst_ref=ref.at[some_rows, pl.ds(SIDE + cols, SIDE), :],
            send_sem=j_send.at[s, t, which],
            recv_sem=j_recv.at[s, t, which],
            device_id={"xline": me_x - 1},
            device_id_type=MESH,
        )
        right = pltpu.make_async_remote_copy(
            src_ref=ref.at[some_rows, pl.ds(cols, SIDE), :],
            dst_ref=ref.at[some_rows, pl.ds(0, SIDE), :],
            send_sem=j_send.at[s, t, which + 1],
            recv_sem=j_recv.at[s, t, which + 1],
            device_id={"xline": me_x + 1},
            device_id_type=MESH,
        )
        return [(has_left, has_right, left), (has_right, has_left, right)]

    def j_tile(s, t):
        return j_copy(s, t, 0, REACH, rows)

    def j_wide(s, t):
        return j_copy(s, t, 0, REACH - EXTRA, rows + 2 * EXTRA)

    started = []

    def start(copies):
        for sends, _, copy in copies:
            pl.when(sends)(copy.start)
        started.extend(copies)

    def await_recv(copies):
        for _, receives, copy in copies:
            pl.when(receives)(copy.wait_recv)

    shot_copies = []

    def to_shot(d, src_ref, dst_ref, send_sem, recv_sem):
        return pltpu.make_async_remote_copy(
            src_ref=src_ref, dst_ref=dst_ref, send_sem=send_sem, recv_sem=recv_sem,
            device_id=partner(d), device_id_type=MESH,
        )

    def field_copy(d, t):
        return to_shot(
            d, fields[0][t].at[tile_rows, tile_cols, :],
            fields[shots - d][t].at[tile_rows, tile_cols, :],
            now_send.at[d, t], now_recv.at[shots - d, t])

    def surf_copy(d):
        return to_shot(d, surf.at[0], surf.at[shots - d], surf_send.at[d],
                       surf_recv.at[shots - d])

    def src_copy(d, t):
        return to_shot(d, src.at[0, t], src.at[shots - d, t], src_send.at[d, t],
                       src_recv.at[shots - d, t])

    def to_shots(copy_of, *what):
        for d in range(1, shots):
            copy = copy_of(d, *what)
            copy.start()
            shot_copies.append(copy)

    @pl.when(jnp.logical_not(has_low))
    def _():
        zero = jnp.zeros((REACH, cols, depth), jnp.float32)
        vel2[0:REACH] = zero
        fields[0][0][0:REACH, tile_cols, :] = zero
        for s in range(shots):
            for t in range(1, steps + 1):
                upto = REACH if t < 3 else REACH - EXTRA
                fields[s][t][0:upto, tile_cols, :] = zero[:upto]

    @pl.when(jnp.logical_not(has_high))
    def _():
        zero = jnp.zeros((REACH, cols, depth), jnp.float32)
        vel2[pl.ds(REACH + rows, REACH)] = zero
        fields[0][0][pl.ds(REACH + rows, REACH), tile_cols, :] = zero
        for s in range(shots):
            for t in range(1, steps + 1):
                upto = REACH if t < 3 else REACH - EXTRA
                fields[s][t][pl.ds(2 * REACH + rows - upto, upto), tile_cols, :] = zero[:upto]

    def zero_side(begin):
        zero = jnp.zeros((rows + 2 * EXTRA, SIDE, depth), jnp.float32)
        for s in range(shots):
            for t in range(steps):
                fields[s][t][pl.ds(REACH - EXTRA, rows + 2 * EXTRA), pl.ds(begin, SIDE), :] = zero

    @pl.when(jnp.logical_not(has_left))
    def _():
        zero_side(0)

    @pl.when(jnp.logical_not(has_right))
    def _():
        zero_side(SIDE + cols)

    pl.semaphore_wait(
        barrier,
        has_low.astype(jnp.int32) + has_high.astype(jnp.int32)
        + has_left.astype(jnp.int32) + has_right.astype(jnp.int32) + (shots - 1),
    )
    loads[0].wait()
    start(z_near(0, 0))
    start(j_tile(0, 0))

    for load in loads[6:]:
        load.wait()
    at_inline, at_xline = src_at_inline[0], src_at_xline[0]
    cell_cols = me_x * cols + lax.broadcasted_iota(jnp.int32, (cols, depth), 0)
    col_inside = (jnp.abs(cell_cols - at_xline) <= mute_reach).astype(jnp.float32)

    def mute(t):
        def mute_row(i, carry):
            hit = (jnp.abs(me_in * rows + i - at_inline) <= mute_reach).astype(jnp.float32)
            src[0, t, i] = src[0, t, i] * (1.0 - hit * col_inside)
            return carry

        lax.fori_loop(0, rows, mute_row, 0)

    mute(0)
    to_shots(src_copy, 0)
    for load in loads[1:6]:
        load.wait()
    start(z_vel())

    col_ids = me_x * cols + lax.broadcasted_iota(jnp.int32, (cols, 1), 0)
    hit_cols = (rec_xline[...] == col_ids).astype(jnp.float32)

    def surface(tile):
        row_ids = (me_in + tile - 1) * rows + lax.broadcasted_iota(jnp.int32, (rows, 1), 0)
        hit_rows = (rec_inline[...] == row_ids).astype(jnp.float32)
        weighted = jnp.concatenate(
            [hit_rows * residual[t : t + 1, :] for t in range(steps)], axis=0
        )
        surf[0, tile] = lax.dot_general(
            hit_cols, weighted, (((1,), (1,)), ((), ())),
            precision=lax.Precision.HIGHEST, preferred_element_type=jnp.float32,
        )

    surface(1)

    lanes = lax.broadcasted_iota(jnp.int32, (cols, depth), 1)

    def advance(s, t, extra):
        now, new = fields[s][t], fields[s][t + 1]

        def one_row(at, tile, i):
            centre = now[at, tile_cols, :]
            total = 3.0 * stencil_weights[0] * centre
            for reach in range(1, 5):
                up = jnp.where(lanes >= reach, pltpu.roll(centre, reach, 1), 0.0)
                down = jnp.where(
                    lanes < depth - reach, pltpu.roll(centre, depth - reach, 1), 0.0)
                total = total + stencil_weights[reach] * (
                    (now[at + reach, tile_cols, :] + now[at - reach, tile_cols, :])
                    + (now[at, pl.ds(SIDE + reach, cols), :]
                       + now[at, pl.ds(SIDE - reach, cols), :])
                    + (up + down))
            shift = lax.rem(receiver_depth - (t * rows + i) + 2 * depth, depth)
            injected = jnp.where(
                lanes == receiver_depth, pltpu.roll(surf[s, tile], shift, 1), 0.0)
            before = older0[i] if t == 0 else fields[s][t - 1][at, tile_cols, :]
            new[at, tile_cols, :] = 2.0 * centre - before + vel2[at] * (total + injected)

        def some_rows(b, carry):
            begin = REACH - extra + b * 4
            tile = begin // rows
            for i in range(4):
                one_row(begin + i, tile, begin - tile * rows + i)
            return carry

        lax.fori_loop(0, (rows + 2 * extra) // 4, some_rows, 0)

    own_count = NLAG // shots
    first_lag = me_shot * own_count

    def correlate(t):
        last = t == steps

        def one_row(i, carry):
            sources = [src[s, t - 1, i] for s in range(shots)]
            for k in range(own_count):
                lag = lags[first_lag + k]
                at = REACH + i + lag
                total = sources[0] * fields[0][t][at, tile_cols, :]
                for s in range(1, shots):
                    total = total + sources[s] * fields[s][t][at, tile_cols, :]
                if t > 1:
                    total = out[k, i] + total
                if last:
                    total = total * jnp.abs(lag).astype(jnp.float32)
                out[k, i] = total
            return carry

        lax.fori_loop(0, rows, one_row, 0)

    await_recv(j_tile(0, 0))
    await_recv(z_near(0, 0))
    advance(0, 0, 0)
    start(z_near(0, 1))
    start(j_tile(0, 1))
    start(z_far(0, 1))
    to_shots(field_copy, 1)
    surface(0)
    surface(2)
    to_shots(surf_copy)
    mute(1)
    to_shots(src_copy, 1)
    await_recv(j_tile(0, 1))
    await_recv(z_near(0, 1))
    advance(0, 1, 0)
    start(z_near(0, 2))
    start(z_far(0, 2))
    to_shots(field_copy, 2)
    for t in range(2, steps):
        mute(t)
        to_shots(src_copy, t)

    for t in (1, 2):
        for s in range(1, shots):
            field_copy(shots - s, t).wait_recv()
            start(z_near(s, t))
            start(z_far(s, t))
    await_recv(z_far(0, 1))
    await_recv(z_near(0, 2))
    await_recv(z_far(0, 2))
    start(j_wide(0, 2))
    await_recv(z_vel())

    for t in range(2, steps):
        for s in range(shots):
            if t == 2 and s > 0:
                for early in (1, 2):
                    await_recv(z_near(s, early))
                    await_recv(z_far(s, early))
                start(j_wide(s, t))
                surf_copy(shots - s).wait_recv()
            await_recv(j_wide(s, t))
            if t > 2:
                await_recv(z_near(s, t))
            advance(s, t, EXTRA)
            start(z_near(s, t + 1))
            if t + 1 < steps:
                start(j_wide(s, t + 1))
        for s in range(1, shots):
            src_copy(shots - s, t - 2).wait_recv()
        correlate(t - 1)
    for t in (steps - 1, steps):
        for s in range(1, shots):
            src_copy(shots - s, t - 1).wait_recv()
        if t == steps:
            for s in range(shots):
                await_recv(z_near(s, t))
        correlate(t)

    for sends, _, copy in started:
        pl.when(sends)(copy.wait_send)
    for copy in shot_copies:
        copy.wait_send()


def on_device(
    sizes,
    vel2,
    adj_prev,
    adj_now,
    src_field,
    residual,
    rec_inline,
    rec_xline,
    src_inline,
    src_xline,
    lag_list,
):
    shots, _, _, rows, cols, depth, steps = sizes
    receivers = residual.shape[-1]
    anywhere = pl.BlockSpec(memory_space=pl.ANY)
    field = pltpu.VMEM((rows + 2 * REACH, cols + 2 * SIDE, depth), jnp.float32)
    dma = pltpu.SemaphoreType.DMA
    return pl.pallas_call(
        functools.partial(kernel, sizes),
        out_shape=jax.ShapeDtypeStruct((NLAG // shots, rows, cols, depth), jnp.float32),
        in_specs=[anywhere] * 10,
        out_specs=pl.BlockSpec(memory_space=pltpu.VMEM),
        scratch_shapes=[field] * (shots * (steps + 1)) + [
            pltpu.SMEM((NLAG,), jnp.int32),
            pltpu.SMEM((1,), jnp.int32),
            pltpu.SMEM((1,), jnp.int32),
            pltpu.VMEM((rows + 2 * REACH, cols, depth), jnp.float32),
            pltpu.VMEM((rows, cols, depth), jnp.float32),
            pltpu.VMEM((steps, receivers), jnp.float32),
            pltpu.VMEM((1, receivers), jnp.int32),
            pltpu.VMEM((1, receivers), jnp.int32),
            pltpu.VMEM((shots, steps, rows, cols, depth), jnp.float32),
            pltpu.VMEM((shots, 3, cols, steps * rows), jnp.float32),
            dma((10,)),
            dma((2,)), dma((2,)),
            dma((shots,)), dma((shots,)),
            dma((shots, 3)), dma((shots, 3)),
            dma((shots, steps)), dma((shots, steps)),
            dma((shots, steps + 1, 4)), dma((shots, steps + 1, 4)),
            dma((shots, steps + 1, 2)), dma((shots, steps + 1, 2)),
        ],
        compiler_params=pltpu.CompilerParams(
            collective_id=0, has_side_effects=True, vmem_limit_bytes=52 * 2**20),
        name="adjoint_window",
    )(lag_list, src_inline, src_xline, vel2, adj_prev, adj_now, residual, rec_inline, rec_xline,
      src_field)


def solution(mesh):
    in_specs = (
        P("inline", "xline", None),
        P(("group", "shot"), "inline", "xline", None),
        P(("group", "shot"), "inline", "xline", None),
        P(("group", "shot"), None, "inline", "xline", None),
        P(("group", "shot"), None, None),
        P(("group", "shot"), None),
        P(("group", "shot"), None),
        P(("group", "shot")),
        P(("group", "shot")),
        P(),
    )
    out_specs = P(("group", "shot"), "inline", "xline", None)

    def whole(vel2, adj_prev, adj_now, src_field, *rest):
        n_inline, n_xline = mesh.shape["inline"], mesh.shape["xline"]
        sizes = (mesh.shape["shot"], n_inline, n_xline, vel2.shape[0] // n_inline,
                 vel2.shape[1] // n_xline, vel2.shape[2], src_field.shape[1])
        return jax.shard_map(
            functools.partial(on_device, sizes), mesh=mesh, in_specs=in_specs,
            out_specs=out_specs, check_vma=False,
        )(vel2, adj_prev, adj_now, src_field, *rest)

    return whole
```

time: 72.8 us -> 67.5 us (0.927)
  Pallas kernels: 61.3 us -> 55.9 us
    pallas_call x1, Pallas kernels: 61.3 us -> 55.9 us  [on_device(): pl.pallas_call(functools.partial(kernel, sizes), out_shape=jax.ShapeDtype...]
where the time goes in v2:
time: 67.5 us; the launch traced here: 67.1 us
  Pallas kernels  55.9 us (83%)
  local copies, waits for them, and re-layouts  9.81 us (15%)
  between operations  1.32 us (2%)
    pallas_call x1, Pallas kernels, on_device(): pl.pallas_call(functools.partial(kernel, sizes), out_shape=jax.ShapeDtype...  55.9 us
    unnamed x17, local copies, waits for them, and re-layouts  9.81 us

profile of v2, /device:TPU:0, one launch (start us, length us, event | category | flops | bytes accessed | tf_op | source)
XLA Modules:
  0.0 67.1 jit_solution(5844627934806105054)
XLA Ops:
  1.3 0.0 copy-start
  1.3 1.2 %copy-done = f32[1,8,16,16,128]{4,3,2,1,0:T(8,128)S(1)} copy-done((f32[1,8,16,16,128]{4,3,2,1,0:T(8,128)S(1)}, f32[1,8,16,16,128]{4,3,2,1,0:T(8,128)}, u32[]{:S(2)}) %copy-start) | copy-done | bytes 1048600
  2.5 0.0 copy-start.1
  2.5 0.9 %copy-done.1 = f32[16,16,128]{2,1,0:T(8,128)S(1)} copy-done((f32[16,16,128]{2,1,0:T(8,128)S(1)}, f32[16,16,128]{2,1,0:T(8,128)}, u32[]{:S(2)}) %copy-start.1) | copy-done | bytes 131096
  3.4 0.0 copy-start.2
  3.4 0.9 %copy-done.2 = f32[1,16,16,128]{3,2,1,0:T(8,128)S(1)} copy-done((f32[1,16,16,128]{3,2,1,0:T(8,128)S(1)}, f32[1,16,16,128]{3,2,1,0:T(8,128)}, u32[]{:S(2)}) %copy-start.2) | copy-done | bytes 131096
  4.3 0.0 copy-start.3
  4.3 0.9 %copy-done.3 = f32[1,16,16,128]{3,2,1,0:T(8,128)S(1)} copy-done((f32[1,16,16,128]{3,2,1,0:T(8,128)S(1)}, f32[1,16,16,128]{3,2,1,0:T(8,128)}, u32[]{:S(2)}) %copy-start.3) | copy-done | bytes 131096
  5.2 0.0 copy-start.4
  5.2 0.8 %copy-done.4 = f32[1,8,1024]{2,1,0:T(8,128)S(1)} copy-done((f32[1,8,1024]{2,1,0:T(8,128)S(1)}, f32[1,8,1024]{2,1,0:T(8,128)}, u32[]{:S(2)}) %copy-start.4) | copy-done | bytes 32792
  6.0 0.0 copy-start.5
  6.0 0.7 %copy-done.5 = s32[1,1024]{1,0:T(1,128)S(1)} copy-done((s32[1,1024]{1,0:T(1,128)S(1)}, s32[1,1024]{1,0:T(1,128)}, u32[]{:S(2)}) %copy-start.5) | copy-done | bytes 4120
  6.7 0.0 copy-start.6
  6.7 0.7 %copy-done.6 = s32[1,1024]{1,0:T(1,128)S(1)} copy-done((s32[1,1024]{1,0:T(1,128)S(1)}, s32[1,1024]{1,0:T(1,128)}, u32[]{:S(2)}) %copy-start.6) | copy-done | bytes 4120
  7.4 0.0 copy-start.7
  7.4 0.7 copy-done.7
  8.0 55.9 %adjoint_window.1 = f32[16,16,16,128]{3,2,1,0:T(8,128)} custom-call(s32[32]{0:T(128)S(1)} %copy-done.7, s32[1]{0:T(128)S(6)} %copy.12.src_at_inline_in, s32[1]{0:T(128)S(6)} %copy.13.src_at_xline_in, f32[16,16,128]{2,1,0:T(8,128)S(1)} %copy-done.1, f32[1,16,16,128]{3,2,1,0:T(8,128)S(1)} %copy-done.2, f32[1,16,16,128]{3,2,1,0:T(8,128)S(1)} %copy-done.3, ...), custom_call_target="tpu_custom_call" | custom-call | tf_op jit(solution)/shard_map/adjoint_window/pallas_call | solution.py:417
  64.0 3.1 %copy.14 = f32[16,16,16,128]{3,2,1,0:T(8,128)} copy(f32[16,16,16,128]{3,2,1,0:T(8,128)} %adjoint_window.1) | data formatting | bytes 4194304
Async XLA Ops:
  1.3 1.2 %copy-start = (f32[1,8,16,16,128]{4,3,2,1,0:T(8,128)S(1)}, f32[1,8,16,16,128]{4,3,2,1,0:T(8,128)}, u32[]{:S(2)}) copy-start(f32[1,8,16,16,128]{4,3,2,1,0:T(8,128)} %src_field.1) | copy-start | bytes 3145732
  2.5 0.9 %copy-start.1 = (f32[16,16,128]{2,1,0:T(8,128)S(1)}, f32[16,16,128]{2,1,0:T(8,128)}, u32[]{:S(2)}) copy-start(f32[16,16,128]{2,1,0:T(8,128)} %vel2_in.1) | copy-start | bytes 393220
  3.4 0.9 %copy-start.2 = (f32[1,16,16,128]{3,2,1,0:T(8,128)S(1)}, f32[1,16,16,128]{3,2,1,0:T(8,128)}, u32[]{:S(2)}) copy-start(f32[1,16,16,128]{3,2,1,0:T(8,128)} %adj_prev_in.1) | copy-start | bytes 393220
  4.3 0.9 %copy-start.3 = (f32[1,16,16,128]{3,2,1,0:T(8,128)S(1)}, f32[1,16,16,128]{3,2,1,0:T(8,128)}, u32[]{:S(2)}) copy-start(f32[1,16,16,128]{3,2,1,0:T(8,128)} %adj_now_in.1) | copy-start | bytes 393220
  5.2 0.8 %copy-start.4 = (f32[1,8,1024]{2,1,0:T(8,128)S(1)}, f32[1,8,1024]{2,1,0:T(8,128)}, u32[]{:S(2)}) copy-start(f32[1,8,1024]{2,1,0:T(8,128)} %residual_in.1) | copy-start | bytes 98308
  6.0 0.7 %copy-start.5 = (s32[1,1024]{1,0:T(1,128)S(1)}, s32[1,1024]{1,0:T(1,128)}, u32[]{:S(2)}) copy-start(s32[1,1024]{1,0:T(1,128)} %rec_inline_in.1) | copy-start | bytes 12292
  6.7 0.7 %copy-start.6 = (s32[1,1024]{1,0:T(1,128)S(1)}, s32[1,1024]{1,0:T(1,128)}, u32[]{:S(2)}) copy-start(s32[1,1024]{1,0:T(1,128)} %rec_xline_in.1) | copy-start | bytes 12292
  7.4 0.7 copy-start.7

commit v3 on v2

--- a/solution.py
+++ b/solution.py
@@ -155,8 +155,12 @@
     def j_tile(s, t):
         return j_copy(s, t, 0, REACH, rows)
 
-    def j_wide(s, t):
-        return j_copy(s, t, 0, REACH - EXTRA, rows + 2 * EXTRA)
+    def j_inner(s, t):
+        return j_copy(s, t, 0, REACH - EXTRA + NEAR, rows + 2 * (EXTRA - NEAR))
+
+    def j_outer(s, t):
+        return (j_copy(s, t, 2, REACH - EXTRA, NEAR)
+                + j_copy(s, t, 4, REACH + rows + EXTRA - NEAR, NEAR))
 
     started = []
 
@@ -258,7 +262,6 @@
     to_shots(src_copy, 0)
     for load in loads[1:6]:
         load.wait()
-    start(z_vel())
 
     col_ids = me_x * cols + lax.broadcasted_iota(jnp.int32, (cols, 1), 0)
     hit_cols = (rec_xline[...] == col_ids).astype(jnp.float32)
@@ -278,7 +281,7 @@
 
     lanes = lax.broadcasted_iota(jnp.int32, (cols, depth), 1)
 
-    def advance(s, t, extra):
+    def advance(s, t, begin_row, end_row):
         now, new = fields[s][t], fields[s][t + 1]
 
         def one_row(at, tile, i):
@@ -300,13 +303,13 @@
             new[at, tile_cols, :] = 2.0 * centre - before + vel2[at] * (total + injected)
 
         def some_rows(b, carry):
-            begin = REACH - extra + b * 4
+            begin = b * 4
             tile = begin // rows
             for i in range(4):
                 one_row(begin + i, tile, begin - tile * rows + i)
             return carry
 
-        lax.fori_loop(0, (rows + 2 * extra) // 4, some_rows, 0)
+        lax.fori_loop(begin_row // 4, end_row // 4, some_rows, 0)
 
     own_count = NLAG // shots
     first_lag = me_shot * own_count
@@ -333,7 +336,7 @@
 
     await_recv(j_tile(0, 0))
     await_recv(z_near(0, 0))
-    advance(0, 0, 0)
+    advance(0, 0, REACH, REACH + rows)
     start(z_near(0, 1))
     start(j_tile(0, 1))
     start(z_far(0, 1))
@@ -341,27 +344,28 @@
     surface(0)
     surface(2)
     to_shots(surf_copy)
-    mute(1)
-    to_shots(src_copy, 1)
     await_recv(j_tile(0, 1))
     await_recv(z_near(0, 1))
-    advance(0, 1, 0)
+    advance(0, 1, REACH, REACH + rows)
     start(z_near(0, 2))
     start(z_far(0, 2))
     to_shots(field_copy, 2)
-    for t in range(2, steps):
+    start(z_vel())
+    for t in range(1, steps):
         mute(t)
-        to_shots(src_copy, t)
 
     for t in (1, 2):
         for s in range(1, shots):
             field_copy(shots - s, t).wait_recv()
             start(z_near(s, t))
             start(z_far(s, t))
+    for t in range(1, steps):
+        to_shots(src_copy, t)
     await_recv(z_far(0, 1))
     await_recv(z_near(0, 2))
     await_recv(z_far(0, 2))
-    start(j_wide(0, 2))
+    start(j_inner(0, 2))
+    start(j_outer(0, 2))
     await_recv(z_vel())
 
     for t in range(2, steps):
@@ -370,15 +374,26 @@
                 for early in (1, 2):
                     await_recv(z_near(s, early))
                     await_recv(z_far(s, early))
-                start(j_wide(s, t))
+                start(j_inner(s, t))
+                start(j_outer(s, t))
                 surf_copy(shots - s).wait_recv()
-            await_recv(j_wide(s, t))
+            await_recv(j_inner(s, t))
+            low, high = REACH - EXTRA, REACH + rows + EXTRA
+            advance(s, t, REACH, REACH + NEAR)
+            advance(s, t, REACH + rows - NEAR, REACH + rows)
+            start(z_near(s, t + 1))
+            advance(s, t, low + NEAR, REACH)
+            advance(s, t, REACH + NEAR, REACH + rows - NEAR)
+            advance(s, t, REACH + rows, high - NEAR)
+            if t + 1 < steps:
+                start(j_inner(s, t + 1))
+            await_recv(j_outer(s, t))
             if t > 2:
                 await_recv(z_near(s, t))
-            advance(s, t, EXTRA)
-            start(z_near(s, t + 1))
+            advance(s, t, low, low + NEAR)
+            advance(s, t, high - NEAR, high)
             if t + 1 < steps:
-                start(j_wide(s, t + 1))
+                start(j_outer(s, t + 1))
         for s in range(1, shots):
             src_copy(shots - s, t - 2).wait_recv()
         correlate(t - 1)
@@ -436,10 +451,10 @@
             dma((shots, 3)), dma((shots, 3)),
             dma((shots, steps)), dma((shots, steps)),
             dma((shots, steps + 1, 4)), dma((shots, steps + 1, 4)),
-            dma((shots, steps + 1, 2)), dma((shots, steps + 1, 2)),
+            dma((shots, steps + 1, 6)), dma((shots, steps + 1, 6)),
         ],
         compiler_params=pltpu.CompilerParams(
-            collective_id=0, has_side_effects=True, vmem_limit_bytes=52 * 2**20),
+            collective_id=0, has_side_effects=True, vmem_limit_bytes=63 * 2**20),
         name="adjoint_window",
     )(lag_list, src_inline, src_xline, vel2, adj_prev, adj_now, residual, rec_inline, rec_xline,
       src_field)

time: 67.5 us -> 53.7 us (0.80)
  Pallas kernels: 55.9 us -> 49.1 us
  local copies, waits for them, and re-layouts: 9.81 us -> 3.1 us
    pallas_call x1, Pallas kernels: 55.9 us -> 49.1 us  [on_device(): pl.pallas_call(functools.partial(kernel, sizes), out_shape=jax.ShapeDtype...]
    unnamed x17 -> x1, local copies, waits for them, and re-layouts: 9.81 us -> 3.1 us
where the time goes in v3:
time: 53.7 us; the launch traced here: 53.5 us
  Pallas kernels  49.1 us (91%)
  local copies, waits for them, and re-layouts  3.1 us (6%)
  between operations  1.3 us (2%)
    pallas_call x1, Pallas kernels, on_device(): pl.pallas_call(functools.partial(kernel, sizes), out_shape=jax.ShapeDtype...  49.1 us
    unnamed x1, local copies, waits for them, and re-layouts  3.1 us

profile of v3, /device:TPU:0, one launch (start us, length us, event | category | flops | bytes accessed | tf_op | source)
XLA Modules:
  0.0 53.5 jit_solution(15266616927272866078)
XLA Ops:
  1.3 49.1 %adjoint_window.1 = f32[16,16,16,128]{3,2,1,0:T(8,128)} custom-call(s32[32]{0:T(128)} %lags_in.1, s32[1]{0:T(128)S(6)} %copy.12.src_at_inline_in, s32[1]{0:T(128)S(6)} %copy.13.src_at_xline_in, f32[16,16,128]{2,1,0:T(8,128)} %vel2_in.1, f32[1,16,16,128]{3,2,1,0:T(8,128)} %adj_prev_in.1, f32[1,16,16,128]{3,2,1,0:T(8,128)} %adj_now_in.1, ...), custom_call_target="tpu_custom_call" | custom-call | tf_op jit(solution)/shard_map/adjoint_window/pallas_call | solution.py:432
  50.4 3.1 %copy.14 = f32[16,16,16,128]{3,2,1,0:T(8,128)} copy(f32[16,16,16,128]{3,2,1,0:T(8,128)} %adjoint_window.1) | data formatting | bytes 4194304

commit v4 on v3

--- a/solution.py
+++ b/solution.py
@@ -281,7 +281,7 @@
 
     lanes = lax.broadcasted_iota(jnp.int32, (cols, depth), 1)
 
-    def advance(s, t, begin_row, end_row):
+    def advance(s, t, blocks, begin_of):
         now, new = fields[s][t], fields[s][t + 1]
 
         def one_row(at, tile, i):
@@ -303,13 +303,13 @@
             new[at, tile_cols, :] = 2.0 * centre - before + vel2[at] * (total + injected)
 
         def some_rows(b, carry):
-            begin = b * 4
+            begin = begin_of(b)
             tile = begin // rows
             for i in range(4):
                 one_row(begin + i, tile, begin - tile * rows + i)
             return carry
 
-        lax.fori_loop(begin_row // 4, end_row // 4, some_rows, 0)
+        lax.fori_loop(0, blocks, some_rows, 0)
 
     own_count = NLAG // shots
     first_lag = me_shot * own_count
@@ -336,7 +336,7 @@
 
     await_recv(j_tile(0, 0))
     await_recv(z_near(0, 0))
-    advance(0, 0, REACH, REACH + rows)
+    advance(0, 0, rows // 4, lambda b: REACH + 4 * b)
     start(z_near(0, 1))
     start(j_tile(0, 1))
     start(z_far(0, 1))
@@ -346,7 +346,7 @@
     to_shots(surf_copy)
     await_recv(j_tile(0, 1))
     await_recv(z_near(0, 1))
-    advance(0, 1, REACH, REACH + rows)
+    advance(0, 1, rows // 4, lambda b: REACH + 4 * b)
     start(z_near(0, 2))
     start(z_far(0, 2))
     to_shots(field_copy, 2)
@@ -379,19 +379,15 @@
                 surf_copy(shots - s).wait_recv()
             await_recv(j_inner(s, t))
             low, high = REACH - EXTRA, REACH + rows + EXTRA
-            advance(s, t, REACH, REACH + NEAR)
-            advance(s, t, REACH + rows - NEAR, REACH + rows)
+            advance(s, t, 2, lambda b: REACH + b * (rows - NEAR))
             start(z_near(s, t + 1))
-            advance(s, t, low + NEAR, REACH)
-            advance(s, t, REACH + NEAR, REACH + rows - NEAR)
-            advance(s, t, REACH + rows, high - NEAR)
+            advance(s, t, 6, lambda b: low + NEAR + 4 * b + 4 * (b // 2))
             if t + 1 < steps:
                 start(j_inner(s, t + 1))
             await_recv(j_outer(s, t))
             if t > 2:
                 await_recv(z_near(s, t))
-            advance(s, t, low, low + NEAR)
-            advance(s, t, high - NEAR, high)
+            advance(s, t, 2, lambda b: low + b * (high - NEAR - low))
             if t + 1 < steps:
                 start(j_outer(s, t + 1))
         for s in range(1, shots):

time: 53.7 us -> 55.7 us (1.037)
  Pallas kernels: 49.1 us -> 51.1 us
    pallas_call x1, Pallas kernels: 49.1 us -> 51.1 us  [on_device(): pl.pallas_call(functools.partial(kernel, sizes), out_shape=jax.ShapeDtype...]
where the time goes in v4:
time: 55.7 us; the launch traced here: 55.5 us
  Pallas kernels  51.1 us (92%)
  local copies, waits for them, and re-layouts  3.1 us (6%)
  between operations  1.3 us (2%)
    pallas_call x1, Pallas kernels, on_device(): pl.pallas_call(functools.partial(kernel, sizes), out_shape=jax.ShapeDtype...  51.1 us
    unnamed x1, local copies, waits for them, and re-layouts  3.1 us

profile of v4, /device:TPU:0, one launch (start us, length us, event | category | flops | bytes accessed | tf_op | source)
XLA Modules:
  0.0 55.5 jit_solution(17043001452682909495)
XLA Ops:
  1.3 51.1 %adjoint_window.1 = f32[16,16,16,128]{3,2,1,0:T(8,128)} custom-call(s32[32]{0:T(128)} %lags_in.1, s32[1]{0:T(128)S(6)} %copy.12.src_at_inline_in, s32[1]{0:T(128)S(6)} %copy.13.src_at_xline_in, f32[16,16,128]{2,1,0:T(8,128)} %vel2_in.1, f32[1,16,16,128]{3,2,1,0:T(8,128)} %adj_prev_in.1, f32[1,16,16,128]{3,2,1,0:T(8,128)} %adj_now_in.1, ...), custom_call_target="tpu_custom_call" | custom-call | tf_op jit(solution)/shard_map/adjoint_window/pallas_call | solution.py:428
  52.4 3.1 %copy.14 = f32[16,16,16,128]{3,2,1,0:T(8,128)} copy(f32[16,16,16,128]{3,2,1,0:T(8,128)} %adjoint_window.1) | data formatting | bytes 4194304
